TPU v7x, 128 devices: a whole 4x4x4 slice. The times are simulated.
128 devices in a mesh: blk: 16 (over x_lo, y, core), sp: 8 (over x_hi, z).
Axes of the slice: x: 4 (x_hi: 2, x_lo: 2; x = x_hi * 2 + x_lo), y: 4, z: 4, core: 2. Of those that a mesh axis runs over, the one named last changes fastest.
Arguments:
- query: bfloat16 [33280, 256], P(('blk', 'sp')), may hold values from -6 to 6
- keys: bfloat16 [33280, 256], P(('blk', 'sp')), may hold values from -6 to 6
- values: bfloat16 [33280, 256], P(('blk', 'sp')), may hold values from -6 to 6
Outputs:
- attended: bfloat16 [33280, 256], P(('blk', 'sp'))
All inputs are finite; a program needn't handle non-finite values.
Results may differ from a plain program's by a relative error of at most 0.01.
Values may be sent and summed in bfloat16 or wider, within the bound.
A program may use at most 128 MiB of HBM per device.

v0:
```python
import math

import jax
import jax.numpy as jnp
from jax import lax
from jax.sharding import PartitionSpec as P

HEADS = 2


def local(query, keys, values):
    tok_rows = query.shape[0]
    head_size = query.shape[1] // HEADS
    score_scale = head_size ** (-0.5)
    queries = query.reshape(tok_rows, HEADS, head_size)
    starting = (
        jnp.full((HEADS, tok_rows), -jnp.inf, jnp.float32),
        jnp.zeros((HEADS, tok_rows), jnp.float32),
        jnp.zeros((tok_rows, HEADS, head_size), jnp.float32),
    )

    def advance(running, key_value):
        row_max, totals, mixed_sum = running
        key_block, value_block = key_value
        scores = (
            jnp.einsum("qhd,khd->hqk", queries, key_block, preferred_element_type=jnp.float32)
            * score_scale
        )
        new_max = jnp.maximum(row_max, jnp.max(scores, axis=-1))
        shrink = jnp.exp(row_max - new_max)
        weights = jnp.exp(scores - new_max[:, :, None])
        totals = totals * shrink + jnp.sum(weights, axis=-1)
        mixed_sum = mixed_sum * jnp.transpose(shrink)[:, :, None] + jnp.einsum(
            "hqk,khd->qhd",
            weights.astype(jnp.bfloat16),
            value_block,
            preferred_element_type=jnp.float32,
        )
        return ((new_max, totals, mixed_sum), None)

    frame_keys, frame_values = (
        lax.all_gather(keys, "sp", axis=0, tiled=True),
        lax.all_gather(values, "sp", axis=0, tiled=True),
    )
    key_rows = lax.all_gather(frame_keys, "blk", axis=0, tiled=True)
    value_rows = lax.all_gather(frame_values, "blk", axis=0, tiled=True)
    key_count = key_rows.shape[0]
    block_len = math.gcd(key_count, 8 * tok_rows)
    key_blocks = key_rows.reshape(key_count // block_len, block_len, HEADS, head_size)
    value_blocks = value_rows.reshape(key_count // block_len, block_len, HEADS, head_size)
    row_max, totals, mixed_sum = lax.scan(advance, starting, (key_blocks, value_blocks))[0]
    attended = (mixed_sum / jnp.transpose(totals)[:, :, None]).astype(jnp.bfloat16)
    return attended.reshape(tok_rows, HEADS * head_size)


def solution(mesh):
    return jax.shard_map(
        local,
        mesh=mesh,
        in_specs=(P(("blk", "sp"), None), P(("blk", "sp"), None), P(("blk", "sp"), None)),
        out_specs=P(("blk", "sp"), None),
        check_vma=False,
    )
```

profile of v0, /device:TPU:1, one launch (start us, length us, event | category | flops | bytes accessed | tf_op | source)
XLA Modules:
  0.0 508.7 jit_solution(1539682343323750085)
XLA Ops:
  8.1 50.3 %all-gather.11.cloned.1.call-done = bf16[8,260,256]{2,1,0:T(8,128)(2,1)} async-done(((bf16[1,260,256]{2,1,0:T(8,128)(2,1)}), bf16[8,260,256]{2,1,0:T(8,128)(2,1)}) %all-gather.11.cloned.1.call-update) | async-done | bytes 1064976 | tf_op jit(solution)/shard_map/all_gather | solution.py:42
  60.6 45.6 %all-gather.13.cloned.1.call-done = bf16[8,260,256]{2,1,0:T(8,128)(2,1)} async-done(((bf16[1,260,256]{2,1,0:T(8,128)(2,1)}), bf16[8,260,256]{2,1,0:T(8,128)(2,1)}) %all-gather.13.cloned.1.call-update) | async-done | bytes 1064976 | tf_op jit(solution)/shard_map/all_gather | solution.py:43
  108.5 92.7 %all-gather.7.cloned.1.call-done = bf16[33280,256]{1,0:T(8,128)(2,1)} async-done(((bf16[2080,256]{1,0:T(8,128)(2,1)}), bf16[33280,256]{1,0:T(8,128)(2,1)}) %all-gather.7.cloned.1.call-update) | async-done | bytes 17039376 | tf_op jit(solution)/shard_map/all_gather | solution.py:45
  201.1 32.4 %reshape.23 = bf16[16,2080,2,128]{3,2,1,0:T(2,128)(2,1)} reshape(bf16[33280,256]{1,0:T(8,128)(2,1)} %all-gather.7.cloned.1.call-done) | data formatting | bytes 34078720 | tf_op jit(solution)/shard_map/reshape | solution.py:49
  233.5 63.0 %all-gather.9.cloned.1.call-done = bf16[33280,256]{1,0:T(8,128)(2,1)} async-done(((bf16[2080,256]{1,0:T(8,128)(2,1)}), bf16[33280,256]{1,0:T(8,128)(2,1)}) %all-gather.9.cloned.1.call-update) | async-done | bytes 17039376 | tf_op jit(solution)/shard_map/all_gather | solution.py:46
  296.5 32.3 %reshape.24 = bf16[16,2080,2,128]{3,2,1,0:T(2,128)(2,1)} reshape(bf16[33280,256]{1,0:T(8,128)(2,1)} %all-gather.9.cloned.1.call-done) | data formatting | bytes 34078720 | tf_op jit(solution)/shard_map/reshape | solution.py:50
  328.8 172.3 %while.15 = (s32[]{:T(128)}, f32[2,260]{1,0:T(2,128)S(1)}, f32[2,260]{1,0:T(2,128)S(1)}, f32[260,2,128]{2,0,1:T(8,128)S(1)}, bf16[16,2080,2,128]{3,2,1,0:T(2,128...) while((s32[]{:T(128)}, f32[2,260]{1,0:T(2,128)S(1)}, ...), condition=%wide.region_3.4_spmd.clone, body=%wide.region_0.3_spmd.clone.sunk | while | flops 560471616 | bytes 37373576 | solution.py:51
  335.0 3.4 fusion.31
  339.5 3.2 constant_dynamic-slice_fusion.3
  345.8 3.4 fusion.31
  356.6 3.4 fusion.31
  367.3 3.4 fusion.31
  378.1 3.4 fusion.31
  388.9 3.4 fusion.31
  399.7 3.4 fusion.31
  410.4 3.4 fusion.31
  421.2 3.4 fusion.31
  432.0 3.4 fusion.31
  442.7 3.4 fusion.31
  453.5 3.4 fusion.31
  464.3 3.4 fusion.31
  475.0 3.4 fusion.31
  485.8 3.4 fusion.31
  496.6 3.4 fusion.31
  (148 shorter events, 121.4 us)
Async XLA Ops:
  6.5 101.8 %copy-start.1 = (bf16[260,256]{1,0:T(8,128)(2,1)S(1)}, bf16[260,256]{1,0:T(8,128)(2,1)}, u32[]{:S(2)}) copy-start(bf16[260,256]{1,0:T(8,128)(2,1)} %param.5) | copy-start | bytes 399364
  6.5 51.9 %all-gather.11.cloned.1.call-start = ((), (), s32[]{:S(2)}) async-start(), calls=%async_computation.2 | async-start | bytes 1216512 | tf_op jit(solution)/shard_map/all_gather | solution.py:42
  7.3 98.9 %all-gather.13.cloned.1.call-start = ((), (), s32[]{:S(2)}) async-start(), calls=%async_computation.3 | async-start | bytes 1216512 | tf_op jit(solution)/shard_map/all_gather | solution.py:43
  8.0 193.1 %all-gather.7.cloned.1.call-start = ((), (), s32[]{:S(2)}) async-start(), calls=%async_computation | async-start | bytes 18104320 | tf_op jit(solution)/shard_map/all_gather | solution.py:45
  60.5 236.0 %all-gather.9.cloned.1.call-start = ((), (), s32[]{:S(2)}) async-start(), calls=%async_computation.1 | async-start | bytes 18104320 | tf_op jit(solution)/shard_map/all_gather | solution.py:46
  335.0 3.7 copy-start
  345.8 3.7 copy-start
  356.6 3.7 copy-start
  367.3 3.7 copy-start
  378.1 3.7 copy-start
  388.9 3.7 copy-start
  399.6 3.7 copy-start
  410.4 3.7 copy-start
  421.2 3.7 copy-start
  432.0 3.7 copy-start
  442.7 3.7 copy-start
  453.5 3.7 copy-start
  464.3 3.7 copy-start
  475.0 3.7 copy-start
  485.8 3.7 copy-start
  496.6 3.7 copy-start
Sparse Core Ops, SparseCore 0:
  9.7 48.6 all-gather.10
  60.7 45.4 all-gather.12
  107.9 93.2 all-gather.6
  202.7 93.7 all-gather.8
where the time goes:
time: 511 us; the launch traced here: 509 us
  waiting for transfers between devices  253 us (50%)
  local copies, waits for them, and re-layouts  126 us (25%)
  matrix products  102 us (20%)
  other arithmetic  13.4 us (3%)
  between operations  13.2 us (3%)
    all_gather x1, waiting for transfers between devices, local(): key_rows = lax.all_gather(frame_keys, 'blk', axis=0, tiled=True)  92.7 us
    all_gather x1, waiting for transfers between devices, local(): value_rows = lax.all_gather(frame_values, 'blk', axis=0, tiled=True)  63 us
    dot_general x16, matrix products, advance(): jnp.einsum('hqk,khd->qhd', weights.astype(jnp.bfloat16), value_block, pre...  53.9 us
    dynamic_slice x16, local copies, waits for them, and re-layouts, local(): lax.scan(advance, starting, (key_blocks, value_blocks))[0]  51.2 us
    all_gather x1, waiting for transfers between devices, local(): lax.all_gather(keys, 'sp', axis=0, tiled=True)  50.3 us
    dot_general x16, matrix products, advance(): jnp.einsum('qhd,khd->hqk', queries, key_block, preferred_element_type=jnp...  48.5 us
    all_gather x1, waiting for transfers between devices, local(): lax.all_gather(values, 'sp', axis=0, tiled=True)  45.6 us
    reshape x1, local copies, waits for them, and re-layouts, local(): key_rows.reshape(key_count // block_len, block_len, HEADS, head_size)  32.4 us
  transfers between devices with their start and end apart: 4, of which 4 were waited for; matrix products, arithmetic and copies ran while one was open for 7% of the time, Pallas kernels for 0%

commit v1 on v0

v1 whole, which is shorter than its diff:
```python
import jax
import jax.numpy as jnp
from jax import lax
from jax.experimental import pallas as pl
from jax.experimental.pallas import tpu as pltpu
from jax.sharding import PartitionSpec as P

MESH = pl.DeviceIdType.MESH
HEADS = 2
HEAD = 128
ROWS = 260
FULL = 256
PAD = 272
PAIR = 2 * PAD
LOG2E = 1.4426950408889634
FACTOR = HEAD**-0.5 * LOG2E

NEAR = (0, 1, 2, 3, 4, 5, 8, 9)
FAR = (6, 7, 10, 11, 12, 13, 14, 15)
SECOND = ((1, 1, 0), (2, 1, 0), (2, 2, 0), (1, 4, 1), (0, 4, 1), (0, 2, 1))
THIRD = ((2, 3, 0), (0, 6, 1))


def place():
    blk, sp = lax.axis_index("blk"), lax.axis_index("sp")
    return (2 * (sp // 4) + blk // 8, (blk // 2) % 4, sp % 4), blk % 2


def device(chip, core):
    x, y, z = chip
    return ((x % 2) * 8 + y * 2 + core, (x // 2) * 4 + z)


def pair_even(a):
    return a + 1 - 2 * (a % 2)


def pair_odd(a):
    return (a + 3 + 2 * (a % 2)) % 4


def neighbour(chip, axis, pair):
    return tuple(pair(a) if n == axis else a for n, a in enumerate(chip))


def kernel(
    q_ref, k_ref, v_ref, out_ref,
    kv_mine, q_mine, kv_held, q_held, peak, mixed, wide_a, wide_b, top_a, top_b,
    part, lse, got, got_lse,
    kv_send, kv_recv, q_send, q_recv, part_send, part_recv, lse_send, lse_recv,
):
    chip, core = place()
    sibling = device(chip, 1 - core)

    def stage(ref, store, head):
        cols = pl.ds(pl.multiple_of(head * HEAD, HEAD), HEAD)
        store(0, FULL, ref[0:FULL, cols])
        store(FULL, PAD, ref[0 : PAD - FULL, cols])
        store(FULL, ROWS, ref[FULL:ROWS, cols])

    def into(ref, lanes, slot=None):
        def store(lo, hi, rows):
            if slot is None:
                ref[lo:hi, lanes] = rows
            else:
                ref[slot, lo:hi, lanes] = rows

        return store

    low, high = slice(0, HEAD), slice(HEAD, 2 * HEAD)
    stage(q_ref, into(q_held, low, core), core)
    stage(k_ref, into(kv_held, low, core), core)
    stage(v_ref, into(kv_held, high, core), core)
    stage(q_ref, into(q_mine, low), 1 - core)
    stage(k_ref, into(kv_mine, low), 1 - core)
    stage(v_ref, into(kv_mine, high), 1 - core)
    pads = jnp.zeros((PAD - ROWS, HEAD), jnp.bfloat16)
    kv_held[core, ROWS:PAD, high] = pads
    kv_mine[ROWS:PAD, high] = pads

    barrier = pltpu.get_barrier_semaphore()
    pl.semaphore_signal(barrier, inc=1, device_id=sibling, device_id_type=MESH)
    for pair in (pair_odd, pair_even):
        for axis in range(3):
            pl.semaphore_signal(
                barrier, inc=1, device_id=device(neighbour(chip, axis, pair), core), device_id_type=MESH
            )
    pl.semaphore_wait(barrier, 7)

    sends = []

    def send(kind, axis, offset, c):
        held, send_sem, recv_sem, pair = kind
        slot, there = 2 * offset + c, 2 * (offset + 2**axis) + c
        copy = pltpu.make_async_remote_copy(
            held.at[slot], held.at[there], send_sem.at[there], recv_sem.at[there],
            device_id=device(neighbour(chip, axis, pair), core), device_id_type=MESH,
        )
        copy.start()
        sends.append(copy)

    def cross(kind, mine):
        held, send_sem, recv_sem, pair = kind
        copy = pltpu.make_async_remote_copy(
            mine, held.at[core], send_sem.at[0], recv_sem.at[core], device_id=sibling, device_id_type=MESH
        )
        copy.start()
        sends.append(copy)

    def arrive(kind, slot):
        held, send_sem, recv_sem, pair = kind
        pltpu.make_async_copy(held.at[slot], held.at[slot], recv_sem.at[slot]).wait()

    q_kind = (q_held, q_send, q_recv, pair_odd)
    kv_kind = (kv_held, kv_send, kv_recv, pair_even)
    cross(q_kind, q_mine)
    cross(kv_kind, kv_mine)
    for axis in range(3):
        send(q_kind, axis, 0, core)
        send(kv_kind, axis, 0, core)
    arrive(q_kind, 1 - core)
    for axis in range(3):
        send(q_kind, axis, 0, 1 - core)
    arrive(kv_kind, 1 - core)
    for axis in range(3):
        send(kv_kind, axis, 0, 1 - core)
    seen = set()

    def forward(kind, steps):
        for axis, offset, c in steps:
            if (id(kind), offset, c) not in seen:
                seen.add((id(kind), offset, c))
                arrive(kind, 2 * offset + c)
            send(kind, axis, offset, c)

    def rest(kind, slots):
        for slot in slots:
            if slot > 1 and (id(kind), slot // 2, slot % 2) not in seen:
                seen.add((id(kind), slot // 2, slot % 2))
                arrive(kind, slot)

    forward(q_kind, SECOND)
    forward(kv_kind, SECOND)
    forward(q_kind, THIRD)
    rest(q_kind, range(16))
    rest(kv_kind, NEAR)

    def keys_of(slots, tails):
        rows = [kv_held[s, 0:FULL, low] for s in slots]
        if tails:
            rows += [kv_held[s, FULL:PAD, low] for s in range(16)]
        keys = jnp.concatenate(rows, axis=0)
        return jnp.concatenate([keys, keys], axis=1)

    def values_of(slots, tails):
        rows = [kv_held[s, 0:FULL, high] for s in slots]
        ones = jnp.ones((FULL * len(slots), HEAD), jnp.bfloat16)
        if tails:
            rows += [kv_held[s, FULL:PAD, high] for s in range(16)]
            row = lax.broadcasted_iota(jnp.int32, (16 * (PAD - FULL), HEAD), 0)
            real = jnp.where(row % (PAD - FULL) < ROWS - FULL, 1.0, 0.0).astype(jnp.bfloat16)
            ones = jnp.concatenate([ones, real], axis=0)
        return jnp.concatenate([jnp.concatenate(rows, axis=0), ones], axis=1)

    def rows_of(t):
        return pl.ds(pl.multiple_of(t * PAIR, 16), PAIR)

    def score(t, slots, tails, wide, top):
        q = q_held[pl.ds(2 * t, 2)].reshape(PAIR, HEAD).astype(jnp.float32) * FACTOR
        q_high = q.astype(jnp.bfloat16)
        q_low = (q - q_high.astype(jnp.float32)).astype(jnp.bfloat16)
        s = lax.dot_general(
            jnp.concatenate([q_high, q_low], axis=1), keys_of(slots, tails),
            (((1,), (1,)), ((), ())), preferred_element_type=jnp.float32,
        )
        width = s.shape[1]
        wide[:, 0:width] = s
        most = s[:, 0:HEAD]
        for j in range(HEAD, width, HEAD):
            most = jnp.maximum(most, s[:, j : j + HEAD])
        top[...] = jnp.broadcast_to(jnp.max(most, axis=1, keepdims=True), (PAIR, HEAD))

    def mix(slots, tails, wide, peaks):
        width = FULL * len(slots) + (16 * (PAD - FULL) if tails else 0)
        weights = jnp.exp2(wide[:, 0:width] - jnp.concatenate([peaks] * (width // HEAD), axis=1))
        return jnp.dot(weights.astype(jnp.bfloat16), values_of(slots, tails), preferred_element_type=jnp.float32)

    def first(t, wide, top):
        peaks = top[...]
        peak[rows_of(t), :] = peaks
        mixed[rows_of(t), :] = mix(NEAR, False, wide, peaks)

    def last(t, wide, top):
        before = peak[rows_of(t), :]
        peaks = jnp.maximum(before, top[...])
        shrink = jnp.exp2(before - peaks)
        total = mixed[rows_of(t), :] * jnp.concatenate([shrink, shrink], axis=1) + mix(FAR, True, wide, peaks)
        sums = total[:, HEAD:]
        part[pl.ds(2 * t, 2)] = (total[:, 0:HEAD] / sums).astype(jnp.bfloat16).reshape(2, PAD, HEAD)
        logs = peaks + jnp.log2(sums)
        pick = jnp.where(lax.broadcasted_iota(jnp.int32, (8, HEAD), 1) == 0, 1.0, 0.0)
        for c in range(2):
            lse[2 * t + c, :, 0:PAD] = lax.dot_general(
                pick, logs[c * PAD : (c + 1) * PAD], (((1,), (1,)), ((), ())),
                preferred_element_type=jnp.float32, precision=lax.Precision.HIGHEST,
            )

    def result_copies(t, c):
        owner = tuple(a + ((t // 2**n) % 2) * (pair_odd(a) - a) for n, a in enumerate(chip))
        here, there = 2 * t + c, 2 * t + core
        return [
            pltpu.make_async_remote_copy(
                src.at[here], dst.at[there], send_sem.at[here], recv_sem.at[there],
                device_id=device(owner, c), device_id_type=MESH,
            )
            for src, dst, send_sem, recv_sem in (
                (part, got, part_send, part_recv), (lse, got_lse, lse_send, lse_recv)
            )
        ]

    def post(t):
        for c in range(2):
            for copy in result_copies(t, c):
                copy.start()

    bufs = ((wide_a, top_a), (wide_b, top_b))

    def near_score(t, b):
        score(t, NEAR, False, *bufs[b])

    def far_score(t, b):
        score(t, FAR, True, *bufs[b])

    near_score(0, 0)

    def near_step(i, _):
        near_score(2 * i + 1, 1)
        first(2 * i, *bufs[0])
        near_score(2 * i + 2, 0)
        first(2 * i + 1, *bufs[1])
        return 0

    lax.fori_loop(0, 2, near_step, 0)
    forward(kv_kind, THIRD)
    lax.fori_loop(2, 3, near_step, 0)
    near_score(7, 1)
    first(6, *bufs[0])
    rest(kv_kind, FAR)
    far_score(7, 0)
    first(7, *bufs[1])

    def far_step(i, _):
        t = 7 - 2 * i
        far_score(t - 1, 1)
        last(t, *bufs[0])
        post(t)
        far_score(t - 2, 0)
        last(t - 1, *bufs[1])
        post(t - 1)
        return 0

    lax.fori_loop(0, 3, far_step, 0)
    far_score(0, 1)
    last(1, *bufs[0])
    post(1)
    last(0, *bufs[1])
    crossing = result_copies(0, 1 - core)
    for copy in crossing:
        copy.start()
    got[core] = part[core]
    got_lse[core] = lse[core]

    for slot in range(16):
        for kind, recv in ((got, part_recv), (got_lse, lse_recv)):
            if slot < 2:
                continue
            pltpu.make_async_copy(kind.at[slot], kind.at[slot], recv.at[slot]).wait()
    for kind, recv in ((got, part_recv), (got_lse, lse_recv)):
        pltpu.make_async_copy(kind.at[1 - core], kind.at[1 - core], recv.at[1 - core]).wait()

    which = lax.broadcasted_iota(jnp.int32, (8, PAD), 0)
    for head in range(2):
        logs = got_lse[head, :, 0:PAD]
        for o in range(1, 8):
            logs = jnp.where(which == o, got_lse[2 * o + head, :, 0:PAD], logs)
        shares = jnp.exp2(logs - jnp.max(logs, axis=0, keepdims=True))
        shares = shares / jnp.sum(shares, axis=0, keepdims=True)
        shares = jnp.transpose(shares)
        result = jnp.zeros((PAD, HEAD), jnp.float32)
        for o in range(8):
            result = result + got[2 * o + head].astype(jnp.float32) * shares[:, o : o + 1]
        out_ref[:, head * HEAD : (head + 1) * HEAD] = result[0:ROWS].astype(jnp.bfloat16)

    for copy in sends:
        copy.wait_send()
    for t in range(1, 8):
        for c in range(2):
            for copy in result_copies(t, c):
                copy.wait_send()
    for copy in crossing:
        copy.wait_send()


def local(query, keys, values):
    vmem = pl.BlockSpec(memory_space=pltpu.VMEM)
    shard = (16, PAD, HEAD)
    widest = FULL * len(FAR) + 16 * (PAD - FULL)
    dma = pltpu.SemaphoreType.DMA((16,))
    return pl.pallas_call(
        kernel,
        out_shape=jax.ShapeDtypeStruct((ROWS, HEADS * HEAD), jnp.bfloat16),
        in_specs=[vmem] * 3,
        out_specs=vmem,
        scratch_shapes=[
            pltpu.VMEM((PAD, 2 * HEAD), jnp.bfloat16),
            pltpu.VMEM((PAD, HEAD), jnp.bfloat16),
            pltpu.VMEM((16, PAD, 2 * HEAD), jnp.bfloat16),
            pltpu.VMEM(shard, jnp.bfloat16),
            pltpu.VMEM((16 * PAD, HEAD), jnp.float32),
            pltpu.VMEM((16 * PAD, 2 * HEAD), jnp.float32),
            pltpu.VMEM((PAIR, widest), jnp.float32),
            pltpu.VMEM((PAIR, widest), jnp.float32),
            pltpu.VMEM((PAIR, HEAD), jnp.float32),
            pltpu.VMEM((PAIR, HEAD), jnp.float32),
            pltpu.VMEM(shard, jnp.bfloat16),
            pltpu.VMEM((16, 8, 384), jnp.float32),
            pltpu.VMEM(shard, jnp.bfloat16),
            pltpu.VMEM((16, 8, 384), jnp.float32),
        ]
        + [dma] * 8,
        compiler_params=pltpu.CompilerParams(
            collective_id=0, has_side_effects=True, vmem_limit_bytes=56 * 2**20
        ),
        cost_estimate=pl.CostEstimate(flops=8860000000, bytes_accessed=600000, transcendentals=17300000),
        name="attend",
    )(query, keys, values)


def solution(mesh):
    spec = P(("blk", "sp"), None)
    return jax.shard_map(local, mesh=mesh, in_specs=(spec, spec, spec), out_specs=spec, check_vma=False)
```

time: 511 us -> 63 us (0.12)
  waiting for transfers between devices: 253 us -> 0 us
  local copies, waits for them, and re-layouts: 126 us -> 1.57 us
  matrix products: 102 us -> 0 us
  Pallas kernels: 0 us -> 61.2 us
  other arithmetic: 13.4 us -> 0 us
  between operations: 13.2 us -> 0.01 us
    all_gather x4 -> x0, waiting for transfers between devices: 252 us -> none  [the longest x1 92.7 us: local(): key_rows = lax.all_gather(frame_keys, 'blk', axis=0, tiled=True)]
    dot_general x32 -> x0, matrix products: 102 us -> none  [the longest x16 53.9 us: advance(): jnp.einsum('hqk,khd->qhd', weights.astype(jnp.bfloat16), value_block, pre...]
    reshape x3 -> x0, local copies, waits for them, and re-layouts: 64.7 us -> none  [the longest x1 32.4 us: local(): key_rows.reshape(key_count // block_len, block_len, HEADS, head_size)]
    pallas_call x0 -> x1, Pallas kernels: none -> 61.2 us  [local(): pl.pallas_call(kernel, out_shape=jax.ShapeDtypeStruct((ROWS, HEADS * HEAD...]
    dynamic_slice x16 -> x0, local copies, waits for them, and re-layouts: 51.2 us -> none  [local(): lax.scan(advance, starting, (key_blocks, value_blocks))[0]]
    reduce_sum x16 -> x0, other arithmetic: 12.8 us -> none  [advance(): totals = totals * shrink + jnp.sum(weights, axis=-1)]
  transfers between devices with their start and end apart: 4 -> 0, of which waited for: 4 -> 0; matrix products, arithmetic and copies ran while one was open for 7% -> 0% of each run, Pallas kernels for 0% -> 0%
where the time goes in v1:
time: 63 us; the launch traced here: 62.8 us
  Pallas kernels  61.2 us (97%)
  local copies, waits for them, and re-layouts  1.57 us (2%)
    pallas_call x1, Pallas kernels, local(): pl.pallas_call(kernel, out_shape=jax.ShapeDtypeStruct((ROWS, HEADS * HEAD...  61.2 us
    unnamed x1, local copies, waits for them, and re-layouts  1.57 us

profile of v1, /device:TPU:1, one launch (start us, length us, event | category | flops | bytes accessed | tf_op | source)
XLA Modules:
  0.0 62.8 jit_solution(12158342666425492447)
XLA Ops:
  0.0 61.2 %attend.1 = bf16[260,256]{1,0:T(8,128)(2,1)} custom-call(bf16[260,256]{1,0:T(8,128)(2,1)} %q_ref.1, bf16[260,256]{1,0:T(8,128)(2,1)} %k_ref.1, bf16[260,256]{1,0:T(8,128)(2,1)} %v_ref.1), custom_call_target="tpu_custom_call" | custom-call | flops 8860000256 | bytes 600000 | tf_op jit(solution)/shard_map/attend/pallas_call | solution.py:309
  61.3 1.6 %copy.5 = bf16[260,256]{1,0:T(8,128)(2,1)} copy(bf16[260,256]{1,0:T(8,128)(2,1)} %attend.1) | data formatting | bytes 266240

commit v2 on v1

--- a/solution.py
+++ b/solution.py
@@ -89,23 +89,23 @@
 
     sends = []
 
-    def send(kind, axis, offset, c):
+    def hop(kind, axis, offset, c):
         held, send_sem, recv_sem, pair = kind
         slot, there = 2 * offset + c, 2 * (offset + 2**axis) + c
-        copy = pltpu.make_async_remote_copy(
+        return pltpu.make_async_remote_copy(
             held.at[slot], held.at[there], send_sem.at[there], recv_sem.at[there],
             device_id=device(neighbour(chip, axis, pair), core), device_id_type=MESH,
         )
-        copy.start()
-        sends.append(copy)
+
+    def send(*what):
+        hop(*what).start()
+        sends.append(what)
 
     def cross(kind, mine):
         held, send_sem, recv_sem, pair = kind
-        copy = pltpu.make_async_remote_copy(
+        return pltpu.make_async_remote_copy(
             mine, held.at[core], send_sem.at[0], recv_sem.at[core], device_id=sibling, device_id_type=MESH
         )
-        copy.start()
-        sends.append(copy)
 
     def arrive(kind, slot):
         held, send_sem, recv_sem, pair = kind
@@ -113,8 +113,9 @@
 
     q_kind = (q_held, q_send, q_recv, pair_odd)
     kv_kind = (kv_held, kv_send, kv_recv, pair_even)
-    cross(q_kind, q_mine)
-    cross(kv_kind, kv_mine)
+    crosses = [cross(q_kind, q_mine), cross(kv_kind, kv_mine)]
+    for copy in crosses:
+        copy.start()
     for axis in range(3):
         send(q_kind, axis, 0, core)
         send(kv_kind, axis, 0, core)
@@ -141,9 +142,8 @@
 
     forward(q_kind, SECOND)
     forward(kv_kind, SECOND)
-    forward(q_kind, THIRD)
-    rest(q_kind, range(16))
     rest(kv_kind, NEAR)
+    rest(q_kind, NEAR)
 
     def keys_of(slots, tails):
         rows = [kv_held[s, 0:FULL, low] for s in slots]
@@ -185,6 +185,17 @@
         weights = jnp.exp2(wide[:, 0:width] - jnp.concatenate([peaks] * (width // HEAD), axis=1))
         return jnp.dot(weights.astype(jnp.bfloat16), values_of(slots, tails), preferred_element_type=jnp.float32)
 
+    def across(column):
+        lane = lax.broadcasted_iota(jnp.int32, (HEAD, HEAD), 1)
+        diagonal = lane == lax.broadcasted_iota(jnp.int32, (HEAD, HEAD), 0)
+        row = lax.broadcasted_iota(jnp.int32, (8, HEAD), 0)
+        result = jnp.zeros((8, HEAD), jnp.float32)
+        for n, lo in enumerate(range(0, PAD, HEAD)):
+            rows = min(HEAD, PAD - lo)
+            line = jnp.sum(jnp.where(diagonal[:rows], column[lo : lo + rows], 0.0), axis=0, keepdims=True)
+            result = jnp.where(row == n, line, result)
+        return result
+
     def first(t, wide, top):
         peaks = top[...]
         peak[rows_of(t), :] = peaks
@@ -198,12 +209,8 @@
         sums = total[:, HEAD:]
         part[pl.ds(2 * t, 2)] = (total[:, 0:HEAD] / sums).astype(jnp.bfloat16).reshape(2, PAD, HEAD)
         logs = peaks + jnp.log2(sums)
-        pick = jnp.where(lax.broadcasted_iota(jnp.int32, (8, HEAD), 1) == 0, 1.0, 0.0)
         for c in range(2):
-            lse[2 * t + c, :, 0:PAD] = lax.dot_general(
-                pick, logs[c * PAD : (c + 1) * PAD], (((1,), (1,)), ((), ())),
-                preferred_element_type=jnp.float32, precision=lax.Precision.HIGHEST,
-            )
+            lse[2 * t + c] = across(logs[c * PAD : (c + 1) * PAD])
 
     def result_copies(t, c):
         owner = tuple(a + ((t // 2**n) % 2) * (pair_odd(a) - a) for n, a in enumerate(chip))
@@ -231,18 +238,31 @@
     def far_score(t, b):
         score(t, FAR, True, *bufs[b])
 
+    def near_tile(p):
+        return jnp.where(p == 3, 4, jnp.where(p == 4, 3, p))
+
     near_score(0, 0)
 
     def near_step(i, _):
-        near_score(2 * i + 1, 1)
-        first(2 * i, *bufs[0])
-        near_score(2 * i + 2, 0)
-        first(2 * i + 1, *bufs[1])
+        @pl.when(i == 1)
+        def _():
+            forward(q_kind, THIRD)
+            rest(q_kind, (6, 7))
+
+        @pl.when(i == 2)
+        def _():
+            rest(q_kind, range(14))
+            forward(kv_kind, THIRD[:1])
+
+        near_score(near_tile(2 * i + 1), 1)
+        first(near_tile(2 * i), *bufs[0])
+        near_score(near_tile(2 * i + 2), 0)
+        first(near_tile(2 * i + 1), *bufs[1])
         return 0
 
-    lax.fori_loop(0, 2, near_step, 0)
-    forward(kv_kind, THIRD)
-    lax.fori_loop(2, 3, near_step, 0)
+    lax.fori_loop(0, 3, near_step, 0)
+    forward(kv_kind, THIRD[1:])
+    rest(q_kind, range(16))
     near_score(7, 1)
     first(6, *bufs[0])
     rest(kv_kind, FAR)
@@ -278,21 +298,33 @@
     for kind, recv in ((got, part_recv), (got_lse, lse_recv)):
         pltpu.make_async_copy(kind.at[1 - core], kind.at[1 - core], recv.at[1 - core]).wait()
 
-    which = lax.broadcasted_iota(jnp.int32, (8, PAD), 0)
+    which = lax.broadcasted_iota(jnp.int32, (8, HEAD), 0)
     for head in range(2):
-        logs = got_lse[head, :, 0:PAD]
+        logs = [got_lse[2 * o + head] for o in range(8)]
+        most = logs[0]
         for o in range(1, 8):
-            logs = jnp.where(which == o, got_lse[2 * o + head, :, 0:PAD], logs)
-        shares = jnp.exp2(logs - jnp.max(logs, axis=0, keepdims=True))
-        shares = shares / jnp.sum(shares, axis=0, keepdims=True)
-        shares = jnp.transpose(shares)
+            most = jnp.maximum(most, logs[o])
+        shares = [jnp.exp2(x - most) for x in logs]
+        every = shares[0]
+        for o in range(1, 8):
+            every = every + shares[o]
+        shares = [x / every for x in shares]
+        columns = []
+        for n in range(3):
+            lines = jnp.broadcast_to(shares[0][n : n + 1], (8, HEAD))
+            for o in range(1, 8):
+                lines = jnp.where(which == o, shares[o][n : n + 1], lines)
+            columns.append(jnp.transpose(lines))
+        shares = jnp.concatenate(columns, axis=0)[0:PAD]
         result = jnp.zeros((PAD, HEAD), jnp.float32)
         for o in range(8):
             result = result + got[2 * o + head].astype(jnp.float32) * shares[:, o : o + 1]
         out_ref[:, head * HEAD : (head + 1) * HEAD] = result[0:ROWS].astype(jnp.bfloat16)
 
-    for copy in sends:
+    for copy in crosses:
         copy.wait_send()
+    for what in sends:
+        hop(*what).wait_send()
     for t in range(1, 8):
         for c in range(2):
             for copy in result_copies(t, c):
@@ -323,9 +355,9 @@
             pltpu.VMEM((PAIR, HEAD), jnp.float32),
             pltpu.VMEM((PAIR, HEAD), jnp.float32),
             pltpu.VMEM(shard, jnp.bfloat16),
-            pltpu.VMEM((16, 8, 384), jnp.float32),
+            pltpu.VMEM((16, 8, HEAD), jnp.float32),
             pltpu.VMEM(shard, jnp.bfloat16),
-            pltpu.VMEM((16, 8, 384), jnp.float32),
+            pltpu.VMEM((16, 8, HEAD), jnp.float32),
         ]
         + [dma] * 8,
         compiler_params=pltpu.CompilerParams(

time: 63 us -> 52.5 us (0.83)
  Pallas kernels: 61.2 us -> 50.7 us
    pallas_call x1, Pallas kernels: 61.2 us -> 50.7 us  [local(): pl.pallas_call(kernel, out_shape=jax.ShapeDtypeStruct((ROWS, HEADS * HEAD...]
where the time goes in v2:
time: 52.5 us; the launch traced here: 52.3 us
  Pallas kernels  50.7 us (97%)
  local copies, waits for them, and re-layouts  1.57 us (3%)
    pallas_call x1, Pallas kernels, local(): pl.pallas_call(kernel, out_shape=jax.ShapeDtypeStruct((ROWS, HEADS * HEAD...  50.7 us
    unnamed x1, local copies, waits for them, and re-layouts  1.57 us

profile of v2, /device:TPU:1, one launch (start us, length us, event | category | flops | bytes accessed | tf_op | source)
XLA Modules:
  0.0 52.3 jit_solution(12136629009169334321)
XLA Ops:
  0.0 50.7 %attend.1 = bf16[260,256]{1,0:T(8,128)(2,1)} custom-call(bf16[260,256]{1,0:T(8,128)(2,1)} %q_ref.1, bf16[260,256]{1,0:T(8,128)(2,1)} %k_ref.1, bf16[260,256]{1,0:T(8,128)(2,1)} %v_ref.1), custom_call_target="tpu_custom_call" | custom-call | flops 8860000256 | bytes 600000 | tf_op jit(solution)/shard_map/attend/pallas_call | solution.py:341
  50.8 1.6 %copy.5 = bf16[260,256]{1,0:T(8,128)(2,1)} copy(bf16[260,256]{1,0:T(8,128)(2,1)} %attend.1) | data formatting | bytes 266240

commit v3 on v2

v3 whole, which is shorter than its diff:
```python
import jax
import jax.numpy as jnp
from jax import lax
from jax.experimental import pallas as pl
from jax.experimental.pallas import tpu as pltpu
from jax.sharding import PartitionSpec as P

MESH = pl.DeviceIdType.MESH
HEADS = 2
HEAD = 128
ROWS = 260
FULL = 256
PAD = 272
PART = 264
PAIR = 2 * PART
LOG2E = 1.4426950408889634
FACTOR = HEAD**-0.5 * LOG2E

NEAR = (0, 1, 2, 3, 4, 5, 8, 9)
FAR = (6, 7, 10, 11, 12, 13, 14, 15)

def place():
    blk, sp = lax.axis_index("blk"), lax.axis_index("sp")
    return (2 * (sp // 4) + blk // 8, (blk // 2) % 4, sp % 4), blk % 2


def device(chip, core):
    x, y, z = chip
    return ((x % 2) * 8 + y * 2 + core, (x // 2) * 4 + z)


def pair_even(a):
    return a + 1 - 2 * (a % 2)


def pair_odd(a):
    return (a + 3 + 2 * (a % 2)) % 4


def neighbour(chip, axes, pair):
    return tuple(pair(a) if n in axes else a for n, a in enumerate(chip))


def kernel(
    q_ref, k_ref, v_ref, out_ref,
    kv_mine, q_mine, kv_held, q_held, peak, mixed, wide_a, wide_b, top_a, top_b,
    part, got,
    kv_send, kv_recv, q_send, q_recv, part_send, part_recv,
):
    chip, core = place()
    sibling = device(chip, 1 - core)

    barrier = pltpu.get_barrier_semaphore()
    pl.semaphore_signal(barrier, inc=1, device_id=sibling, device_id_type=MESH)
    for pair in (pair_odd, pair_even):
        for axis in range(3):
            pl.semaphore_signal(
                barrier, inc=1, device_id=device(neighbour(chip, (axis,), pair), core), device_id_type=MESH
            )

    def stage(ref, store, head):
        cols = pl.ds(pl.multiple_of(head * HEAD, HEAD), HEAD)
        store(0, FULL, ref[0:FULL, cols])
        store(FULL, PAD, ref[0 : PAD - FULL, cols])
        store(FULL, ROWS, ref[FULL:ROWS, cols])

    def into(ref, lanes, slot=None):
        def store(lo, hi, rows):
            if slot is None:
                ref[lo:hi, lanes] = rows
            else:
                ref[slot, lo:hi, lanes] = rows

        return store

    low, high = slice(0, HEAD), slice(HEAD, 2 * HEAD)
    stage(q_ref, into(q_held, low, core), core)
    stage(k_ref, into(kv_held, low, core), core)
    stage(v_ref, into(kv_held, high, core), core)
    stage(q_ref, into(q_mine, low), 1 - core)
    stage(k_ref, into(kv_mine, low), 1 - core)
    stage(v_ref, into(kv_mine, high), 1 - core)
    pads = jnp.zeros((PAD - ROWS, HEAD), jnp.bfloat16)
    kv_held[core, ROWS:PAD, high] = pads
    kv_mine[ROWS:PAD, high] = pads

    pl.semaphore_wait(barrier, 7)

    sends = []
    early, late = core, 1 - core

    def hop(kind, axes, offset, c):
        held, send_sem, recv_sem, pair = kind
        slot, there = 2 * offset + c, 2 * (offset + sum(2**axis for axis in axes)) + c
        return pltpu.make_async_remote_copy(
            held.at[slot], held.at[there], send_sem.at[there], recv_sem.at[there],
            device_id=device(neighbour(chip, axes, pair), core), device_id_type=MESH,
        )

    def send(*what):
        hop(*what).start()
        sends.append(what)

    def cross(kind, mine):
        held, send_sem, recv_sem, pair = kind
        return pltpu.make_async_remote_copy(
            mine, held.at[core], send_sem.at[core], recv_sem.at[core], device_id=sibling, device_id_type=MESH
        )

    def arrive(kind, offset, c):
        held, send_sem, recv_sem, pair = kind
        slot = 2 * offset + c
        pltpu.make_async_copy(held.at[slot], held.at[slot], recv_sem.at[slot]).wait()

    def own(kind, c):
        for axis in range(3):
            send(kind, (axis,), 0, c)

    def forward(kind, c):
        for axis in range(3):
            arrive(kind, 2**axis, c)
        for axis in range(3):
            send(kind, (axis,), 2 ** ((axis + 1) % 3), c)

    def corner(kind):
        arrive(kind, 6, early)
        send(kind, (0,), 6, early)
        send(kind, (1, 2), 1, late)

    q_kind = (q_held, q_send, q_recv, pair_odd)
    kv_kind = (kv_held, kv_send, kv_recv, pair_even)
    crosses = [cross(q_kind, q_mine), cross(kv_kind, kv_mine)]
    for copy in crosses:
        copy.start()
    own(q_kind, early)
    own(kv_kind, early)
    arrive(q_kind, 0, late)
    own(q_kind, late)
    arrive(kv_kind, 0, late)
    own(kv_kind, late)
    forward(q_kind, early)
    forward(kv_kind, early)
    forward(q_kind, late)
    forward(kv_kind, late)

    def keys_of(slots, tails):
        rows = [kv_held[s, 0:FULL, low] for s in slots]
        if tails:
            rows += [kv_held[s, FULL:PAD, low] for s in range(16)]
        keys = jnp.concatenate(rows, axis=0)
        return jnp.concatenate([keys, keys], axis=1)

    def values_of(slots, tails):
        rows = [kv_held[s, 0:FULL, high] for s in slots]
        ones = jnp.ones((FULL * len(slots), HEAD), jnp.bfloat16)
        if tails:
            rows += [kv_held[s, FULL:PAD, high] for s in range(16)]
            row = lax.broadcasted_iota(jnp.int32, (16 * (PAD - FULL), HEAD), 0)
            real = jnp.where(row % (PAD - FULL) < ROWS - FULL, 1.0, 0.0).astype(jnp.bfloat16)
            ones = jnp.concatenate([ones, real], axis=0)
        return jnp.concatenate([jnp.concatenate(rows, axis=0), ones], axis=1)

    def rows_of(t):
        return pl.ds(pl.multiple_of(t * PAIR, 16), PAIR)

    def score(t, slots, tails, wide, top):
        q = jnp.concatenate([q_held[2 * t + c].astype(jnp.float32)[0:PART] for c in range(2)], axis=0) * FACTOR
        q_high = q.astype(jnp.bfloat16)
        q_low = (q - q_high.astype(jnp.float32)).astype(jnp.bfloat16)
        s = lax.dot_general(
            jnp.concatenate([q_high, q_low], axis=1), keys_of(slots, tails),
            (((1,), (1,)), ((), ())), preferred_element_type=jnp.float32,
        )
        width = s.shape[1]
        wide[:, 0:width] = s
        most = s[:, 0:HEAD]
        for j in range(HEAD, width, HEAD):
            most = jnp.maximum(most, s[:, j : j + HEAD])
        top[...] = jnp.broadcast_to(jnp.max(most, axis=1, keepdims=True), (PAIR, HEAD))

    def mix(slots, tails, wide, peaks):
        width = FULL * len(slots) + (16 * (PAD - FULL) if tails else 0)
        weights = jnp.exp2(wide[:, 0:width] - jnp.concatenate([peaks] * (width // HEAD), axis=1))
        return jnp.dot(weights.astype(jnp.bfloat16), values_of(slots, tails), preferred_element_type=jnp.float32)

    def with_logs(block, column):
        lane = lax.broadcasted_iota(jnp.int32, (HEAD, HEAD), 1)
        diagonal = lane == lax.broadcasted_iota(jnp.int32, (HEAD, HEAD), 0)
        row = lax.broadcasted_iota(jnp.int32, (8, HEAD), 0)
        lines = jnp.zeros((8, HEAD), jnp.float32)
        for n, lo in enumerate(range(0, PART, HEAD)):
            rows = min(HEAD, PART - lo)
            line = jnp.sum(jnp.where(diagonal[:rows], column[lo : lo + rows], 0.0), axis=0, keepdims=True)
            lines = jnp.where(row % 3 == n, line, lines)
        one = lines.astype(jnp.bfloat16).astype(jnp.float32)
        two = (lines - one).astype(jnp.bfloat16).astype(jnp.float32)
        three = lines - one - two
        logs = jnp.where(row < 3, one, jnp.where(row < 6, two, three))
        third = jnp.broadcast_to(three[2:3], (8, HEAD))
        return jnp.concatenate([jnp.where(row == 4, third, block), logs], axis=0)

    def logs_of(tile):
        row = lax.broadcasted_iota(jnp.int32, (8, HEAD), 0)
        block, logs = tile[0:8], tile[8:16]
        three = jnp.where(row == 2, pltpu.roll(block, 6, 0), pltpu.roll(logs, 2, 0))
        return logs + pltpu.roll(logs, 5, 0) + three

    def first(t, wide, top):
        peaks = top[...]
        peak[rows_of(t), :] = peaks
        mixed[rows_of(t), :] = mix(NEAR, False, wide, peaks)

    def last(t, wide, top):
        before = peak[rows_of(t), :]
        peaks = jnp.maximum(before, top[...])
        shrink = jnp.exp2(before - peaks)
        total = mixed[rows_of(t), :] * jnp.concatenate([shrink, shrink], axis=1) + mix(FAR, True, wide, peaks)
        sums = total[:, HEAD:]
        result = total[:, 0:HEAD] / sums
        logs = peaks + jnp.log2(sums)
        for c in range(2):
            mine = result[c * PART : (c + 1) * PART]
            part[2 * t + c, 0:FULL] = mine[0:FULL].astype(jnp.bfloat16)
            end = with_logs(mine[FULL:PART], logs[c * PART : (c + 1) * PART])
            part[2 * t + c, FULL:PAD] = end.astype(jnp.bfloat16)

    def result_copy(t, c):
        owner = tuple(a + ((t // 2**n) % 2) * (pair_odd(a) - a) for n, a in enumerate(chip))
        here, there = 2 * t + c, 2 * t + core
        return pltpu.make_async_remote_copy(
            part.at[here], got.at[there], part_send.at[here], part_recv.at[there],
            device_id=device(owner, c), device_id_type=MESH,
        )

    def post(t):
        for c in range(2):
            result_copy(t, c).start()

    bufs = ((wide_a, top_a), (wide_b, top_b))

    def near_score(t, b):
        score(t, NEAR, False, *bufs[b])

    def far_score(t, b):
        score(t, FAR, True, *bufs[b])

    def near_tile(p):
        return jnp.where(p == 2, 4, jnp.where(p == 3, 3, p + 1))

    near_score(near_tile(0), 0)
    corner(q_kind)

    def near_step(i, _):
        @pl.when(i == 1)
        def _():
            corner(kv_kind)
            arrive(q_kind, 3, early)
            arrive(q_kind, 3, late)

        @pl.when(i == 2)
        def _():
            arrive(q_kind, 6, late)

        near_score(near_tile(2 * i + 1), 1)
        first(near_tile(2 * i), *bufs[0])

        @pl.when(i == 1)
        def _():
            arrive(q_kind, 5, early)
            arrive(q_kind, 5, late)

        @pl.when(i == 2)
        def _():
            arrive(q_kind, 7, early)
            arrive(q_kind, 7, late)

        near_score(near_tile(2 * i + 2), 0)
        first(near_tile(2 * i + 1), *bufs[1])
        return 0

    lax.fori_loop(0, 3, near_step, 0)
    for offset in (3, 5, 6, 7):
        if offset != 6:
            arrive(kv_kind, offset, early)
        arrive(kv_kind, offset, late)
    far_score(7, 1)
    first(7, *bufs[0])

    def far_step(i, _):
        t = 7 - 2 * i
        far_score(t - 1, 0)
        last(t, *bufs[1])
        post(t)
        far_score(t - 2, 1)
        last(t - 1, *bufs[0])
        post(t - 1)
        return 0

    lax.fori_loop(0, 3, far_step, 0)
    near_score(0, 0)
    last(1, *bufs[1])
    post(1)
    far_score(0, 1)
    first(0, *bufs[0])
    last(0, *bufs[1])
    crossing = result_copy(0, 1 - core)
    crossing.start()
    got[core] = part[core]

    for slot in range(2, 16):
        pltpu.make_async_copy(got.at[slot], got.at[slot], part_recv.at[slot]).wait()
    pltpu.make_async_copy(got.at[1 - core], got.at[1 - core], part_recv.at[1 - core]).wait()

    which = lax.broadcasted_iota(jnp.int32, (8, HEAD), 0)
    for head in range(2):
        logs = [logs_of(got[2 * o + head, FULL:PAD].astype(jnp.float32)) for o in range(8)]
        most = logs[0]
        for o in range(1, 8):
            most = jnp.maximum(most, logs[o])
        shares = [jnp.exp2(x - most) for x in logs]
        every = shares[0]
        for o in range(1, 8):
            every = every + shares[o]
        shares = [x / every for x in shares]
        columns = []
        for n in range(3):
            lines = jnp.broadcast_to(shares[0][n : n + 1], (8, HEAD))
            for o in range(1, 8):
                lines = jnp.where(which == o, shares[o][n : n + 1], lines)
            columns.append(jnp.transpose(lines))
        shares = jnp.concatenate(columns, axis=0)[0:PART]
        result = jnp.zeros((PART, HEAD), jnp.float32)
        for o in range(8):
            result = result + got[2 * o + head].astype(jnp.float32)[0:PART] * shares[:, o : o + 1]
        out_ref[:, head * HEAD : (head + 1) * HEAD] = result[0:ROWS].astype(jnp.bfloat16)

    for copy in crosses:
        copy.wait_send()
    for what in sends:
        hop(*what).wait_send()
    for t in range(1, 8):
        for c in range(2):
            result_copy(t, c).wait_send()
    crossing.wait_send()


def local(query, keys, values):
    vmem = pl.BlockSpec(memory_space=pltpu.VMEM)
    shard = (16, PAD, HEAD)
    widest = FULL * len(FAR) + 16 * (PAD - FULL)
    dma = pltpu.SemaphoreType.DMA((16,))
    return pl.pallas_call(
        kernel,
        out_shape=jax.ShapeDtypeStruct((ROWS, HEADS * HEAD), jnp.bfloat16),
        in_specs=[vmem] * 3,
        out_specs=vmem,
        scratch_shapes=[
            pltpu.VMEM((PAD, 2 * HEAD), jnp.bfloat16),
            pltpu.VMEM((PAD, HEAD), jnp.bfloat16),
            pltpu.VMEM((16, PAD, 2 * HEAD), jnp.bfloat16),
            pltpu.VMEM(shard, jnp.bfloat16),
            pltpu.VMEM((8 * PAIR, HEAD), jnp.float32),
            pltpu.VMEM((8 * PAIR, 2 * HEAD), jnp.float32),
            pltpu.VMEM((PAIR, widest), jnp.float32),
            pltpu.VMEM((PAIR, widest), jnp.float32),
            pltpu.VMEM((PAIR, HEAD), jnp.float32),
            pltpu.VMEM((PAIR, HEAD), jnp.float32),
            pltpu.VMEM(shard, jnp.bfloat16),
            pltpu.VMEM(shard, jnp.bfloat16),
        ]
        + [dma] * 6,
        compiler_params=pltpu.CompilerParams(
            collective_id=0, has_side_effects=True, vmem_limit_bytes=56 * 2**20
        ),
        cost_estimate=pl.CostEstimate(flops=8860000000, bytes_accessed=600000, transcendentals=17300000),
        name="attend",
    )(query, keys, values)


def solution(mesh):
    spec = P(("blk", "sp"), None)
    return jax.shard_map(local, mesh=mesh, in_specs=(spec, spec, spec), out_specs=spec, check_vma=False)
```

time: 52.5 us -> 47.9 us (0.912)
  Pallas kernels: 50.7 us -> 46.2 us
    pallas_call x1, Pallas kernels: 50.7 us -> 46.2 us  [local(): pl.pallas_call(kernel, out_shape=jax.ShapeDtypeStruct((ROWS, HEADS * HEAD...]
where the time goes in v3:
time: 47.9 us; the launch traced here: 47.8 us
  Pallas kernels  46.2 us (96%)
  local copies, waits for them, and re-layouts  1.57 us (3%)
    pallas_call x1, Pallas kernels, local(): pl.pallas_call(kernel, out_shape=jax.ShapeDtypeStruct((ROWS, HEADS * HEAD...  46.2 us
    unnamed x1, local copies, waits for them, and re-layouts  1.57 us

profile of v3, /device:TPU:1, one launch (start us, length us, event | category | flops | bytes accessed | tf_op | source)
XLA Modules:
  0.0 47.8 jit_solution(4541680787232632227)
XLA Ops:
  0.0 46.2 %attend.1 = bf16[260,256]{1,0:T(8,128)(2,1)} custom-call(bf16[260,256]{1,0:T(8,128)(2,1)} %q_ref.1, bf16[260,256]{1,0:T(8,128)(2,1)} %k_ref.1, bf16[260,256]{1,0:T(8,128)(2,1)} %v_ref.1), custom_call_target="tpu_custom_call" | custom-call | flops 8860000256 | bytes 600000 | tf_op jit(solution)/shard_map/attend/pallas_call | solution.py:352
  46.2 1.6 %copy.5 = bf16[260,256]{1,0:T(8,128)(2,1)} copy(bf16[260,256]{1,0:T(8,128)(2,1)} %attend.1) | data formatting | bytes 266240

commit v4 on v3

--- a/solution.py
+++ b/solution.py
@@ -12,6 +12,7 @@
 FULL = 256
 PAD = 272
 PART = 264
+TAIL = 128
 PAIR = 2 * PART
 LOG2E = 1.4426950408889634
 FACTOR = HEAD**-0.5 * LOG2E
@@ -52,6 +53,8 @@
 
     barrier = pltpu.get_barrier_semaphore()
     pl.semaphore_signal(barrier, inc=1, device_id=sibling, device_id_type=MESH)
+    diagonal = device(neighbour(chip, (1, 2), pair_even), core)
+    pl.semaphore_signal(barrier, inc=1, device_id=diagonal, device_id_type=MESH)
     for pair in (pair_odd, pair_even):
         for axis in range(3):
             pl.semaphore_signal(
@@ -74,17 +77,25 @@
         return store
 
     low, high = slice(0, HEAD), slice(HEAD, 2 * HEAD)
+    spot = chip[0] % 2 + 2 * (chip[1] % 2)
+    mine = lax.broadcasted_iota(jnp.int32, (PAD - FULL, HEAD), 0) // (ROWS - FULL) == spot
+
+    def stage_keys(ref, store, head):
+        cols = pl.ds(pl.multiple_of(head * HEAD, HEAD), HEAD)
+        store(0, FULL, ref[0:FULL, cols])
+        rest = ref[FULL:ROWS, cols].astype(jnp.float32)
+        for lo in range(0, PAD - FULL, ROWS - FULL):
+            top_a[lo : lo + ROWS - FULL, :] = rest
+        store(FULL, PAD, jnp.where(mine, top_a[0 : PAD - FULL, :], 0.0).astype(jnp.bfloat16))
+
     stage(q_ref, into(q_held, low, core), core)
-    stage(k_ref, into(kv_held, low, core), core)
-    stage(v_ref, into(kv_held, high, core), core)
+    stage_keys(k_ref, into(kv_held, low, core), core)
+    stage_keys(v_ref, into(kv_held, high, core), core)
     stage(q_ref, into(q_mine, low), 1 - core)
-    stage(k_ref, into(kv_mine, low), 1 - core)
-    stage(v_ref, into(kv_mine, high), 1 - core)
-    pads = jnp.zeros((PAD - ROWS, HEAD), jnp.bfloat16)
-    kv_held[core, ROWS:PAD, high] = pads
-    kv_mine[ROWS:PAD, high] = pads
-
-    pl.semaphore_wait(barrier, 7)
+    stage_keys(k_ref, into(kv_mine, low), 1 - core)
+    stage_keys(v_ref, into(kv_mine, high), 1 - core)
+
+    pl.semaphore_wait(barrier, 8)
 
     sends = []
     early, late = core, 1 - core
@@ -122,31 +133,42 @@
         for axis in range(3):
             send(kind, (axis,), 2 ** ((axis + 1) % 3), c)
 
-    def corner(kind):
-        arrive(kind, 6, early)
-        send(kind, (0,), 6, early)
-        send(kind, (1, 2), 1, late)
+    def corner(kind, c):
+        if c is early:
+            arrive(kind, 6, c)
+            send(kind, (0,), 6, c)
+        else:
+            send(kind, (1, 2), 1, c)
 
     q_kind = (q_held, q_send, q_recv, pair_odd)
     kv_kind = (kv_held, kv_send, kv_recv, pair_even)
-    crosses = [cross(q_kind, q_mine), cross(kv_kind, kv_mine)]
+    crosses = [cross(kv_kind, kv_mine), cross(q_kind, q_mine)]
+    own(kv_kind, early)
     for copy in crosses:
         copy.start()
     own(q_kind, early)
-    own(kv_kind, early)
+    arrive(kv_kind, 0, late)
+    own(kv_kind, late)
     arrive(q_kind, 0, late)
     own(q_kind, late)
-    arrive(kv_kind, 0, late)
-    own(kv_kind, late)
     forward(q_kind, early)
     forward(kv_kind, early)
     forward(q_kind, late)
     forward(kv_kind, late)
+    corner(kv_kind, late)
+
+    def packed(lanes):
+        tiles = []
+        for z in range(2):
+            for c in range(2):
+                a, b, d, e = (kv_held[2 * (4 * z + o) + c, FULL:PAD, lanes] for o in range(4))
+                tiles.append((a + b) + (d + e))
+        return jnp.concatenate(tiles, axis=0)
 
     def keys_of(slots, tails):
         rows = [kv_held[s, 0:FULL, low] for s in slots]
         if tails:
-            rows += [kv_held[s, FULL:PAD, low] for s in range(16)]
+            rows += [packed(low)] * 2
         keys = jnp.concatenate(rows, axis=0)
         return jnp.concatenate([keys, keys], axis=1)
 
@@ -154,10 +176,9 @@
         rows = [kv_held[s, 0:FULL, high] for s in slots]
         ones = jnp.ones((FULL * len(slots), HEAD), jnp.bfloat16)
         if tails:
-            rows += [kv_held[s, FULL:PAD, high] for s in range(16)]
-            row = lax.broadcasted_iota(jnp.int32, (16 * (PAD - FULL), HEAD), 0)
-            real = jnp.where(row % (PAD - FULL) < ROWS - FULL, 1.0, 0.0).astype(jnp.bfloat16)
-            ones = jnp.concatenate([ones, real], axis=0)
+            rows += [packed(high), jnp.zeros((TAIL // 2, HEAD), jnp.bfloat16)]
+            half = jnp.ones((TAIL // 2, HEAD), jnp.bfloat16)
+            ones = jnp.concatenate([ones, half, jnp.zeros_like(half)], axis=0)
         return jnp.concatenate([jnp.concatenate(rows, axis=0), ones], axis=1)
 
     def rows_of(t):
@@ -179,7 +200,7 @@
         top[...] = jnp.broadcast_to(jnp.max(most, axis=1, keepdims=True), (PAIR, HEAD))
 
     def mix(slots, tails, wide, peaks):
-        width = FULL * len(slots) + (16 * (PAD - FULL) if tails else 0)
+        width = FULL * len(slots) + (TAIL if tails else 0)
         weights = jnp.exp2(wide[:, 0:width] - jnp.concatenate([peaks] * (width // HEAD), axis=1))
         return jnp.dot(weights.astype(jnp.bfloat16), values_of(slots, tails), preferred_element_type=jnp.float32)
 
@@ -248,12 +269,13 @@
         return jnp.where(p == 2, 4, jnp.where(p == 3, 3, p + 1))
 
     near_score(near_tile(0), 0)
-    corner(q_kind)
+    corner(q_kind, early)
+    corner(q_kind, late)
 
     def near_step(i, _):
         @pl.when(i == 1)
         def _():
-            corner(kv_kind)
+            corner(kv_kind, early)
             arrive(q_kind, 3, early)
             arrive(q_kind, 3, late)
 
@@ -347,7 +369,7 @@
 def local(query, keys, values):
     vmem = pl.BlockSpec(memory_space=pltpu.VMEM)
     shard = (16, PAD, HEAD)
-    widest = FULL * len(FAR) + 16 * (PAD - FULL)
+    widest = FULL * len(FAR) + TAIL
     dma = pltpu.SemaphoreType.DMA((16,))
     return pl.pallas_call(
         kernel,

time: 47.9 us -> 47.9 us (level)
  no operation moved by 1% of the time
where the time goes in v4:
time: 47.9 us; the launch traced here: 47.7 us
  Pallas kernels  46.1 us (96%)
  local copies, waits for them, and re-layouts  1.57 us (3%)
    pallas_call x1, Pallas kernels, local(): pl.pallas_call(kernel, out_shape=jax.ShapeDtypeStruct((ROWS, HEADS * HEAD...  46.1 us
    unnamed x1, local copies, waits for them, and re-layouts  1.57 us

profile of v4, /device:TPU:1, one launch (start us, length us, event | category | flops | bytes accessed | tf_op | source)
XLA Modules:
  0.0 47.7 jit_solution(80152188398288583)
XLA Ops:
  0.0 46.1 %attend.1 = bf16[260,256]{1,0:T(8,128)(2,1)} custom-call(bf16[260,256]{1,0:T(8,128)(2,1)} %q_ref.1, bf16[260,256]{1,0:T(8,128)(2,1)} %k_ref.1, bf16[260,256]{1,0:T(8,128)(2,1)} %v_ref.1), custom_call_target="tpu_custom_call" | custom-call | flops 8860000256 | bytes 600000 | tf_op jit(solution)/shard_map/attend/pallas_call | solution.py:374
  46.2 1.6 %copy.5 = bf16[260,256]{1,0:T(8,128)(2,1)} copy(bf16[260,256]{1,0:T(8,128)(2,1)} %attend.1) | data formatting | bytes 266240
